TPU v7x, 32 devices: a whole 2x2x4 slice. The times are simulated.
32 devices in a mesh: group: 2 (over x), frame: 16 (over z, y, core).
Axes of the slice: x: 2, y: 2, z: 4, core: 2. Of those that a mesh axis runs over, the one named last changes fastest.
Arguments:
- queries: bfloat16 [10240, 5120], P(('group', 'frame')), parts along dimension 0, may hold values from -33 to 33
- keys: bfloat16 [10240, 5120], P(('group', 'frame')), parts along dimension 0, may hold values from -33 to 33
- values: bfloat16 [10240, 5120], P(('group', 'frame')), parts along dimension 0, may hold values from -6 to 6
- labels: int32 [80], P('group'), parts along dimension 0, may hold values from 0 to 1, as said below
- band: int32 [80], P('group'), parts along dimension 0, may hold values from 2 to 4
Outputs:
- attended: bfloat16 [10240, 5120], P(('group', 'frame')), parts along dimension 0
There are 2 independent parts, one for each index of `group`. A program takes and returns all parts, laid end to end along the dimension named above; each array names one. Nothing has to cross between parts.
Inputs may be any that keep to these rules, and one draw needn't show every extreme that they name: `labels`: exactly 10 of the 40 heads carry 1, the others 0.
All inputs are finite; a program needn't handle non-finite values.
Results may differ from a plain program's by a relative error of at most 0.0049.
Values may be sent and summed in bfloat16 or wider, within the bound.
A program may use at most 128 MiB of HBM per device.

v0:
```python
import math

import jax
import jax.numpy as jnp
from jax import lax
from jax.sharding import PartitionSpec as P

TEMP_HEADS = 10


def from_partner(block, axis, bit):
    count = lax.axis_size(axis)
    route = []
    for low in range(count):
        high = low | 1 << bit
        if high != low and high < count:
            route += [(low, high), (high, low)]
    return lax.ppermute(block, axis, route)


def softmax_rounded(scores):
    peak = jnp.max(scores, axis=-1, keepdims=True)
    weights = jnp.exp(scores - peak)
    return (weights / jnp.sum(weights, axis=-1, keepdims=True)).astype(jnp.bfloat16)


def block_heads(count):
    for candidate in (6, 5, 4, 3, 2):
        if count % candidate == 0:
            return candidate
    return 1


def attend_spatial(query_part, key_all, value_all):
    head_total = query_part.shape[1]
    step_heads = block_heads(head_total)
    scale = 1.0 / math.sqrt(query_part.shape[2])

    def one_block(block_number, result):
        start = block_number * step_heads
        query_block = lax.dynamic_slice_in_dim(query_part, start, step_heads, 1)
        key_block = lax.dynamic_slice_in_dim(key_all, start, step_heads, 1)
        value_block = lax.dynamic_slice_in_dim(value_all, start, step_heads, 1)
        scores = (
            jnp.einsum("rhd,khd->hrk", query_block, key_block, preferred_element_type=jnp.float32)
            * scale
        )
        weights = softmax_rounded(scores)
        output_block = jnp.einsum(
            "hrk,khd->rhd", weights, value_block, preferred_element_type=jnp.float32
        ).astype(jnp.bfloat16)
        return lax.dynamic_update_slice_in_dim(result, output_block, start, 1)

    initial = jnp.zeros(query_part.shape, jnp.bfloat16)
    return lax.fori_loop(0, head_total // step_heads, one_block, initial)


def attend_columns(query_part, key_part, value_part, head_band):
    query_cols, key_cols, value_cols = (
        lax.all_to_all(query_part[None], "frame", split_axis=1, concat_axis=0, tiled=True),
        lax.all_to_all(key_part[None], "frame", split_axis=1, concat_axis=0, tiled=True),
        lax.all_to_all(value_part[None], "frame", split_axis=1, concat_axis=0, tiled=True),
    )
    sources, pixels, head_part, head_size = query_cols.shape
    frames = sources // 2
    scale = 1.0 / math.sqrt(head_size)
    grid_shape = (frames, 2, pixels, head_part, head_size)
    scores = (
        jnp.einsum(
            "fapnd,gapnd->apnfg",
            query_cols.reshape(grid_shape),
            key_cols.reshape(grid_shape),
            preferred_element_type=jnp.float32,
        )
        * scale
    )
    frame_ids = jnp.arange(frames, dtype=jnp.int32)
    distance = jnp.abs(frame_ids[:, None] - frame_ids[None, :])
    keep = distance[None, :, :] <= head_band[:, None, None]
    scores = jnp.where(keep, scores, jnp.float32(-1e30))
    weights = softmax_rounded(scores)
    output = jnp.einsum(
        "apnfg,gapnd->fapnd",
        weights,
        value_cols.reshape(grid_shape),
        preferred_element_type=jnp.float32,
    ).astype(jnp.bfloat16)
    output = output.reshape(sources, pixels, head_part, head_size)
    returned = lax.all_to_all(output, "frame", split_axis=0, concat_axis=1, tiled=True)
    return returned[0]


def shards(queries, keys, values, labels, band):
    row_count = queries.shape[0]
    head_count = labels.shape[0]
    head_size = queries.shape[1] // head_count
    query_heads = queries.reshape(row_count, head_count, head_size)
    key_heads = keys.reshape(row_count, head_count, head_size)
    value_heads = values.reshape(row_count, head_count, head_size)
    spatial_count = head_count - TEMP_HEADS
    ordering = jnp.argsort(labels, stable=True)
    spatial_index = ordering[:spatial_count]
    temporal_index = ordering[spatial_count:]
    inverse = jnp.argsort(ordering, stable=True)
    query_spatial = jnp.take(query_heads, spatial_index, axis=1)
    key_spatial = jnp.take(key_heads, spatial_index, axis=1)
    value_spatial = jnp.take(value_heads, spatial_index, axis=1)
    temporal_band = jnp.take(band, temporal_index)
    temporal = attend_columns(
        jnp.take(query_heads, temporal_index, axis=1),
        jnp.take(key_heads, temporal_index, axis=1),
        jnp.take(value_heads, temporal_index, axis=1),
        temporal_band,
    )
    parity = lax.axis_index("frame") % 2
    half = spatial_count // 2
    mine_start = parity * half
    other_start = (1 - parity) * half
    query_mine = lax.dynamic_slice_in_dim(query_spatial, mine_start, half, 1)
    key_mine = lax.dynamic_slice_in_dim(key_spatial, mine_start, half, 1)
    value_mine = lax.dynamic_slice_in_dim(value_spatial, mine_start, half, 1)
    query_other = lax.dynamic_slice_in_dim(query_spatial, other_start, half, 1)
    key_other = lax.dynamic_slice_in_dim(key_spatial, other_start, half, 1)
    value_other = lax.dynamic_slice_in_dim(value_spatial, other_start, half, 1)
    query_got, key_got, value_got = from_partner((query_other, key_other, value_other), "frame", 0)

    def whole_frame(own, got):
        return jnp.where(
            parity == 0, jnp.concatenate([own, got], axis=0), jnp.concatenate([got, own], axis=0)
        )

    frame_out = attend_spatial(
        whole_frame(query_mine, query_got),
        whole_frame(key_mine, key_got),
        whole_frame(value_mine, value_got),
    )
    own_rows = lax.dynamic_slice_in_dim(frame_out, parity * row_count, row_count, 0)
    other_rows = lax.dynamic_slice_in_dim(frame_out, (1 - parity) * row_count, row_count, 0)
    returned = from_partner(other_rows, "frame", 0)
    spatial = jnp.where(
        parity == 0,
        jnp.concatenate([own_rows, returned], axis=1),
        jnp.concatenate([returned, own_rows], axis=1),
    )
    combined = jnp.take(jnp.concatenate([spatial, temporal], axis=1), inverse, axis=1)
    return combined.reshape(row_count, head_count * head_size)


def solution(mesh):
    placed = (
        P(("group", "frame"), None),
        P(("group", "frame"), None),
        P(("group", "frame"), None),
        P("group"),
        P("group"),
    )
    return jax.shard_map(
        shards, mesh=mesh, in_specs=placed, out_specs=P(("group", "frame"), None), check_vma=False
    )
```

profile of v0, /device:TPU:0, one launch (start us, length us, event | category | flops | bytes accessed | tf_op | source)
XLA Modules:
  0.0 211.7 jit_solution(6797831736654225508)
XLA Ops:
  6.7 4.7 %copy_bitcast_fusion = bf16[320,40,128]{2,0,1:T(8,128)(2,1)} fusion(bf16[320,5120]{1,0:T(8,128)(2,1)} %param.12), kind=kLoop, calls=%fused_computation.29 | loop fusion | bytes 6553600 | tf_op jit(solution)/shard_map/reshape | solution.py:98
  13.0 3.5 %gather_fusion.7 = bf16[10,320,128]{2,1,0:T(8,128)(2,1)} fusion(bf16[320,40,128]{2,0,1:T(8,128)(2,1)} %copy_bitcast_fusion, s32[1024]{0:T(1024)S(1)} %pad_clamp_fusion.1), kind=kCustom, calls=%fused_computation.5.clone | custom fusion | bytes 1638440 | tf_op jit(solution)/shard_map/jit(_take)/gather | solution.py:111
  16.5 4.5 %copy_bitcast_fusion.2 = bf16[320,40,128]{2,0,1:T(8,128)(2,1)} fusion(bf16[320,5120]{1,0:T(8,128)(2,1)} %param.13), kind=kLoop, calls=%fused_computation.31 | loop fusion | bytes 6553600 | tf_op jit(solution)/shard_map/reshape | solution.py:99
  21.0 3.5 %gather_fusion.5 = bf16[10,320,128]{2,1,0:T(8,128)(2,1)} fusion(bf16[320,40,128]{2,0,1:T(8,128)(2,1)} %copy_bitcast_fusion.2, s32[1024]{0:T(1024)S(1)} %pad_clamp_fusion.1), kind=kCustom, calls=%fused_computation.1.clone | custom fusion | bytes 1638440 | tf_op jit(solution)/shard_map/jit(_take)/gather | solution.py:112
  29.4 7.4 %all-to-all-start.2 = ((bf16[1,320,10,128]{3,2,0,1:T(8,128)(2,1)}), bf16[1,320,10,128]{3,2,0,1:T(8,128)(2,1)}, u32[]{:S(2)}, u32[]{:S(2)}) async-start(bf16[1,320,10,128]{3,2,0,1:T(8,128)(2,1)} %copy.97), calls=%async_computation.2 | async-start | bytes 2621440 | tf_op jit(solution)/shard_map/all_to_all | solution.py:61
  36.9 4.3 %gather_fusion.4 = bf16[30,320,128]{2,1,0:T(8,128)(2,1)} fusion(bf16[320,40,128]{2,0,1:T(8,128)(2,1)} %copy_bitcast_fusion, s32[1024]{0:T(1024)S(1)} %pad_clamp_fusion.2), kind=kCustom, calls=%fused_computation.3.clone | custom fusion | bytes 4915320 | tf_op jit(solution)/shard_map/jit(_take)/gather | solution.py:106
  43.5 4.4 %gather_fusion.2 = bf16[30,320,128]{2,1,0:T(8,128)(2,1)} fusion(bf16[320,40,128]{2,0,1:T(8,128)(2,1)} %copy_bitcast_fusion.2, s32[1024]{0:T(1024)S(1)} %pad_clamp_fusion.2), kind=kCustom, calls=%fused_computation.clone | custom fusion | bytes 4915320 | tf_op jit(solution)/shard_map/jit(_take)/gather | solution.py:107
  47.9 4.6 %select_bitcast_fusion = (bf16[320,30,128]{2,0,1:T(8,128)(2,1)}, bf16[320,30,128]{2,0,1:T(8,128)(2,1)S(1)}, bf16[320,30,128]{2,0,1:T(8,128)(2,1)S(1)}) fusion(bf16[30,320,128]{2,1,0:T(8,128)(2,1)S(1)} %copy-done.5, pred[30]{0:T(512)(128)(4,1)S(1)} %get-tuple-element.146, bf16[30,320,128]{2,1,0:T(8,128)(2,1)} %gather_fusion.3, ...), kind=kLoop, calls=%fused_computation.37 | loop fusion | flops 3686400 | bytes 14745630 | tf_op jit(solution)/shard_map/jit(_take)/select_n | solution.py:106
  57.9 6.4 %all-to-all-done.2 = bf16[1,320,10,128]{3,2,0,1:T(8,128)(2,1)} async-done(((bf16[1,320,10,128]{3,2,0,1:T(8,128)(2,1)}), bf16[1,320,10,128]{3,2,0,1:T(8,128)(2,1)}, u32[]{:S(2)}, u32[]{:S(2)}) %all-to-all-start.2) | async-done | bytes 819232 | tf_op jit(solution)/shard_map/all_to_all | solution.py:61
  64.3 8.1 %all-to-all-start.1 = ((bf16[1,320,10,128]{3,2,0,1:T(8,128)(2,1)}), bf16[1,320,10,128]{3,2,0,1:T(8,128)(2,1)}, u32[]{:S(2)}, u32[]{:S(2)}) async-start(bf16[1,320,10,128]{3,2,0,1:T(8,128)(2,1)} %copy.94), calls=%async_computation.1 | async-start | bytes 2621440 | tf_op jit(solution)/shard_map/all_to_all | solution.py:60
  78.0 4.0 %maximum_select_fusion = bf16[640,15,128]{2,0,1:T(8,128)(2,1)} fusion(bf16[320,15,128]{2,0,1:T(8,128)(2,1)} %collective-permute-done, bf16[320,15,128]{2,0,1:T(8,128)(2,1)S(1)} %copy-done.8, pred[]{:T(512)S(6)} %eq.4), kind=kLoop, calls=%fused_computation.33 | loop fusion | flops 11059200 | bytes 4915201 | tf_op jit(solution)/shard_map/jit(_where)/select_n | solution.py:128
  82.0 4.0 %maximum_select_fusion.1 = bf16[640,15,128]{2,0,1:T(8,128)(2,1)} fusion(bf16[320,15,128]{2,0,1:T(8,128)(2,1)} %collective-permute-done.1, bf16[320,15,128]{2,0,1:T(8,128)(2,1)S(1)} %copy-done.9, pred[]{:T(512)S(6)} %eq.4), kind=kLoop, calls=%fused_computation.34 | loop fusion | flops 11059200 | bytes 4915201 | tf_op jit(solution)/shard_map/jit(_where)/select_n | solution.py:128
  86.0 3.8 %maximum_select_fusion.2 = bf16[640,15,128]{2,0,1:T(8,128)(2,1)} fusion(bf16[320,15,128]{2,0,1:T(8,128)(2,1)} %collective-permute-done.2, bf16[320,15,128]{2,0,1:T(8,128)(2,1)S(1)} %copy-done.10, pred[]{:T(512)S(6)} %eq.4), kind=kLoop, calls=%fused_computation.35 | loop fusion | flops 11059200 | bytes 4915201 | tf_op jit(solution)/shard_map/jit(_where)/select_n | solution.py:128
  89.8 10.1 %all-to-all-done.1 = bf16[1,320,10,128]{3,2,0,1:T(8,128)(2,1)} async-done(((bf16[1,320,10,128]{3,2,0,1:T(8,128)(2,1)}), bf16[1,320,10,128]{3,2,0,1:T(8,128)(2,1)}, u32[]{:S(2)}, u32[]{:S(2)}) %all-to-all-start.1) | async-done | bytes 819232 | tf_op jit(solution)/shard_map/all_to_all | solution.py:60
  99.9 8.0 %all-to-all-start = ((bf16[1,320,10,128]{3,2,0,1:T(8,128)(2,1)}), bf16[1,320,10,128]{3,2,0,1:T(8,128)(2,1)S(1)}, u32[]{:S(2)}, u32[]{:S(2)}) async-start(bf16[1,320,10,128]{3,2,0,1:T(8,128)(2,1)} %copy.91), calls=%async_computation | async-start | bytes 2621440 | tf_op jit(solution)/shard_map/all_to_all | solution.py:62
  109.8 50.4 %while.13 = (s32[]{:T(128)}, bf16[640,15,128]{2,0,1:T(8,128)(2,1)}, bf16[640,15,128]{2,0,1:T(8,128)(2,1)}, bf16[640,15,128]{2,0,1:T(8,128)(2,1)}, bf16[640,15,12...) while((s32[]{:T(128)}, bf16[640,15,128]{2,0,1:T(8,128)(2,1)}, ...), condition=%wide.region_5.7_spmd, body=%wide.region_2.6_spmd.sunk | while | flops 1067422080 | bytes 72116400 | solution.py:55
  115.6 8.7 %fusion.50 = bf16[640,5,128]{0,2,1:T(8,128)(2,1)S(1)} fusion(f32[5,640]{1,0:T(8,128)S(1)} %fusion.49, bf16[640,15,128]{2,0,1:T(8,128)(2,1)} %get-tuple-element.217, s32[]{:T(128)S(6)} %select_n.164, f32[5,640,640]{1,2,0:T(8,128)} %copy-done.3), kind=kOutput, calls=%fused_computation.16.clone.1 | convolution fusion | flops 534941440 | bytes 18035204 | tf_op jit(solution)/shard_map/while/body/eval_jaxpr/hrk,khd->rhd/dot_general | solution.py:49
  132.4 8.7 %fusion.50 = bf16[640,5,128]{0,2,1:T(8,128)(2,1)S(1)} fusion(f32[5,640]{1,0:T(8,128)S(1)} %fusion.49, bf16[640,15,128]{2,0,1:T(8,128)(2,1)} %get-tuple-element.217, s32[]{:T(128)S(6)} %select_n.164, f32[5,640,640]{1,2,0:T(8,128)} %copy-done.3), kind=kOutput, calls=%fused_computation.16.clone.1 | convolution fusion | flops 534941440 | bytes 18035204 | tf_op jit(solution)/shard_map/while/body/eval_jaxpr/hrk,khd->rhd/dot_general | solution.py:49
  149.2 8.7 %fusion.50 = bf16[640,5,128]{0,2,1:T(8,128)(2,1)S(1)} fusion(f32[5,640]{1,0:T(8,128)S(1)} %fusion.49, bf16[640,15,128]{2,0,1:T(8,128)(2,1)} %get-tuple-element.217, s32[]{:T(128)S(6)} %select_n.164, f32[5,640,640]{1,2,0:T(8,128)} %copy-done.3), kind=kOutput, calls=%fused_computation.16.clone.1 | convolution fusion | flops 534941440 | bytes 18035204 | tf_op jit(solution)/shard_map/while/body/eval_jaxpr/hrk,khd->rhd/dot_general | solution.py:49
  160.2 4.2 %exponential_reduce_fusion = (f32[2,20,10,8]{3,2,1,0:T(8,128)}, f32[2,20,10,8,8]{3,4,2,1,0:T(8,128)S(1)}) fusion(bf16[8,2,20,10,128]{4,3,2,1,0:T(8,128)(2,1)} %bitcast.13, bf16[8,2,20,10,128]{4,3,2,1,0:T(8,128)(2,1)} %bitcast.10, pred[10,8,8]{1,2,0:T(8,128)(4,1)S(1)} %broadcast_compare_fusion), kind=kOutput, calls=%fused_computation.43 | convolution fusion | flops 6656007 | bytes 1754240 | tf_op jit(solution)/shard_map/sub | solution.py:23
  168.8 6.1 %all-to-all-start.3 = ((bf16[16,20,10,128]{3,1,2,0:T(8,128)(2,1)}), bf16[16,20,10,128]{3,1,2,0:T(8,128)(2,1)}, u32[]{:S(2)}, u32[]{:S(2)}) async-start(bf16[16,20,10,128]{3,1,2,0:T(8,128)(2,1)} %copy.104), calls=%async_computation.3 | async-start | bytes 1966080 | tf_op jit(solution)/shard_map/all_to_all | solution.py:89
  183.4 13.4 %all-to-all-done.3 = bf16[16,20,10,128]{3,1,2,0:T(8,128)(2,1)} async-done(((bf16[16,20,10,128]{3,1,2,0:T(8,128)(2,1)}), bf16[16,20,10,128]{3,1,2,0:T(8,128)(2,1)}, u32[]{:S(2)}, u32[]{:S(2)}) %all-to-all-start.3) | async-done | bytes 819232 | tf_op jit(solution)/shard_map/all_to_all | solution.py:89
  202.5 4.9 %gather_fusion.1 = bf16[40,320,128]{2,1,0:T(8,128)(2,1)} fusion(bf16[320,40,128]{2,0,1:T(8,128)(2,1)} %pad_maximum_fusion, s32[1024]{0:T(1024)S(1)} %pad_clamp_fusion), kind=kCustom, calls=%fused_computation.7 | custom fusion | bytes 6553760 | tf_op jit(solution)/shard_map/jit(_take)/gather | solution.py:145
  207.4 4.3 %bitcast_select_fusion = bf16[320,5120]{1,0:T(8,128)(2,1)} fusion(pred[5120]{0:T(1024)(128)(4,1)S(1)} %broadcast_bitcast_fusion, bf16[40,320,128]{2,1,0:T(8,128)(2,1)} %gather_fusion.1), kind=kLoop, calls=%fused_computation.28 | loop fusion | flops 1638400 | bytes 6558720 | tf_op jit(solution)/shard_map/jit(_take)/select_n | solution.py:145
  (88 shorter events, 71.2 us)
Async XLA Ops:
  0.0 1.9 copy-start
  0.0 4.5 %copy-start.13 = (s32[40]{0:T(128)S(1)}, s32[40]{0:T(128)}, u32[]{:S(2)}) copy-start(s32[40]{0:T(128)} %param.14) | copy-start | bytes 484
  6.7 4.7 %copy-start.4 = (bf16[320,40,128]{2,0,1:T(8,128)(2,1)S(1)}, bf16[320,40,128]{2,0,1:T(8,128)(2,1)}, u32[]{:S(2)}) copy-start(bf16[320,40,128]{2,0,1:T(8,128)(2,1)} %copy_bitcast_fusion.1) | copy-start | bytes 9830404
  29.4 34.9 %all-to-all-start.2 = ((bf16[1,320,10,128]{3,2,0,1:T(8,128)(2,1)}), bf16[1,320,10,128]{3,2,0,1:T(8,128)(2,1)}, u32[]{:S(2)}, u32[]{:S(2)}) async-start(bf16[1,320,10,128]{3,2,0,1:T(8,128)(2,1)} %copy.97), calls=%async_computation.2 | async-start | bytes 2621440 | tf_op jit(solution)/shard_map/all_to_all | solution.py:61
  43.5 4.4 %copy-start.5 = (bf16[30,320,128]{2,1,0:T(8,128)(2,1)S(1)}, bf16[30,320,128]{2,1,0:T(8,128)(2,1)}, u32[]{:S(2)}) copy-start(bf16[30,320,128]{2,1,0:T(8,128)(2,1)} %gather_fusion.4) | copy-start | bytes 7372804
  54.1 23.9 %collective-permute-start = (bf16[320,15,128]{2,0,1:T(8,128)(2,1)}, bf16[320,15,128]{2,0,1:T(8,128)(2,1)}, u32[]{:S(2)}, u32[]{:S(2)}) collective-permute-start(bf16[320,15,128]{2,0,1:T(8,128)(2,1)} %get-tuple-element.157), channel_id=1, source_target_pairs={{0,1},{1,0},{2,3},{3,2},{4,5},{5,4},{6,7},{7,6},{8,9},{9,8},{10,11... | collective-permute-start | bytes 3686408 | tf_op jit(solution)/shard_map/ppermute | solution.py:18
  54.5 1.8 copy-start.11
  56.1 16.3 %copy-start.6 = (bf16[320,30,128]{2,0,1:T(8,128)(2,1)S(1)}, bf16[320,30,128]{2,0,1:T(8,128)(2,1)}, u32[]{:S(2)}) copy-start(bf16[320,30,128]{2,0,1:T(8,128)(2,1)} %get-tuple-element.158) | copy-start | bytes 7372804
  56.1 26.0 %collective-permute-start.1 = (bf16[320,15,128]{2,0,1:T(8,128)(2,1)}, bf16[320,15,128]{2,0,1:T(8,128)(2,1)}, u32[]{:S(2)}, u32[]{:S(2)}) collective-permute-start(bf16[320,15,128]{2,0,1:T(8,128)(2,1)} %get-tuple-element.155), channel_id=1, source_target_pairs={{0,1},{1,0},{2,3},{3,2},{4,5},{5,4},{6,7},{7,6},{8,9},{9,8},{10,11... | collective-permute-start | bytes 3686408 | tf_op jit(solution)/shard_map/ppermute | solution.py:18
  64.3 35.5 %all-to-all-start.1 = ((bf16[1,320,10,128]{3,2,0,1:T(8,128)(2,1)}), bf16[1,320,10,128]{3,2,0,1:T(8,128)(2,1)}, u32[]{:S(2)}, u32[]{:S(2)}) async-start(bf16[1,320,10,128]{3,2,0,1:T(8,128)(2,1)} %copy.94), calls=%async_computation.1 | async-start | bytes 2621440 | tf_op jit(solution)/shard_map/all_to_all | solution.py:60
  72.4 4.8 %copy-start.2 = (s32[40]{0:T(128)S(1)}, s32[40]{0:T(128)}, u32[]{:S(2)}) copy-start(s32[40]{0:T(128)} %param.15) | copy-start | bytes 484
  74.1 4.0 %copy-start.8 = (bf16[320,15,128]{2,0,1:T(8,128)(2,1)S(1)}, bf16[320,15,128]{2,0,1:T(8,128)(2,1)}, u32[]{:S(2)}) copy-start(bf16[320,15,128]{2,0,1:T(8,128)(2,1)} %get-tuple-element.156) | copy-start | bytes 3686404
  74.1 11.9 %collective-permute-start.2 = (bf16[320,15,128]{2,0,1:T(8,128)(2,1)}, bf16[320,15,128]{2,0,1:T(8,128)(2,1)}, u32[]{:S(2)}, u32[]{:S(2)}) collective-permute-start(bf16[320,15,128]{2,0,1:T(8,128)(2,1)} %get-tuple-element.153), channel_id=1, source_target_pairs={{0,1},{1,0},{2,3},{3,2},{4,5},{5,4},{6,7},{7,6},{8,9},{9,8},{10,11... | collective-permute-start | bytes 3686408 | tf_op jit(solution)/shard_map/ppermute | solution.py:18
  78.0 4.0 %copy-start.9 = (bf16[320,15,128]{2,0,1:T(8,128)(2,1)S(1)}, bf16[320,15,128]{2,0,1:T(8,128)(2,1)}, u32[]{:S(2)}) copy-start(bf16[320,15,128]{2,0,1:T(8,128)(2,1)} %get-tuple-element.154) | copy-start | bytes 3686404
  82.0 4.0 %copy-start.10 = (bf16[320,15,128]{2,0,1:T(8,128)(2,1)S(1)}, bf16[320,15,128]{2,0,1:T(8,128)(2,1)}, u32[]{:S(2)}) copy-start(bf16[320,15,128]{2,0,1:T(8,128)(2,1)} %get-tuple-element.152) | copy-start | bytes 3686404
  99.9 64.5 %all-to-all-start = ((bf16[1,320,10,128]{3,2,0,1:T(8,128)(2,1)}), bf16[1,320,10,128]{3,2,0,1:T(8,128)(2,1)S(1)}, u32[]{:S(2)}, u32[]{:S(2)}) async-start(bf16[1,320,10,128]{3,2,0,1:T(8,128)(2,1)} %copy.91), calls=%async_computation | async-start | bytes 2621440 | tf_op jit(solution)/shard_map/all_to_all | solution.py:62
  112.4 3.2 %copy-start.3 = (f32[5,640,640]{1,2,0:T(8,128)}, f32[5,640,640]{1,2,0:T(8,128)S(1)}, u32[]{:S(2)}) copy-start(f32[5,640,640]{1,2,0:T(8,128)S(1)} %fusion.48) | copy-start | bytes 24576004 | tf_op jit(solution)/shard_map/while
  129.2 3.2 %copy-start.3 = (f32[5,640,640]{1,2,0:T(8,128)}, f32[5,640,640]{1,2,0:T(8,128)S(1)}, u32[]{:S(2)}) copy-start(f32[5,640,640]{1,2,0:T(8,128)S(1)} %fusion.48) | copy-start | bytes 24576004 | tf_op jit(solution)/shard_map/while
  146.0 3.2 %copy-start.3 = (f32[5,640,640]{1,2,0:T(8,128)}, f32[5,640,640]{1,2,0:T(8,128)S(1)}, u32[]{:S(2)}) copy-start(f32[5,640,640]{1,2,0:T(8,128)S(1)} %fusion.48) | copy-start | bytes 24576004 | tf_op jit(solution)/shard_map/while
  166.2 8.7 %copy-start.7 = (bf16[640,15,128]{2,0,1:T(8,128)(2,1)S(1)}, bf16[640,15,128]{2,0,1:T(8,128)(2,1)}, u32[]{:S(2)}) copy-start(bf16[640,15,128]{2,0,1:T(8,128)(2,1)} %get-tuple-element.105) | copy-start | bytes 7372804
  168.8 28.0 %all-to-all-start.3 = ((bf16[16,20,10,128]{3,1,2,0:T(8,128)(2,1)}), bf16[16,20,10,128]{3,1,2,0:T(8,128)(2,1)}, u32[]{:S(2)}, u32[]{:S(2)}) async-start(bf16[16,20,10,128]{3,1,2,0:T(8,128)(2,1)} %copy.104), calls=%async_computation.3 | async-start | bytes 1966080 | tf_op jit(solution)/shard_map/all_to_all | solution.py:89
  176.5 3.1 %collective-permute-start.3 = (bf16[320,15,128]{2,0,1:T(8,128)(2,1)}, bf16[320,15,128]{2,0,1:T(8,128)(2,1)S(1)}, u32[]{:S(2)}, u32[]{:S(2)}) collective-permute-start(bf16[320,15,128]{2,0,1:T(8,128)(2,1)} %get-tuple-element.151), channel_id=1, source_target_pairs={{0,1},{1,0},{2,3},{3,2},{4,5},{5,4},{6,7},{7,6},{8,9},{9,8},{10,11... | collective-permute-start | bytes 3686408 | tf_op jit(solution)/shard_map/ppermute | solution.py:18
  179.7 1.0 copy-start.12
  202.5 9.2 %copy-start.1 = (bf16[320,5120]{1,0:T(8,128)(2,1)S(1)}, bf16[320,5120]{1,0:T(8,128)(2,1)}, u32[]{:S(2)}) copy-start(bf16[320,5120]{1,0:T(8,128)(2,1)} %param.11) | copy-start | bytes 9830404
where the time goes:
time: 213 us; the launch traced here: 212 us
  local copies, waits for them, and re-layouts  71.1 us (33%)
  matrix products  39.9 us (19%)
  other arithmetic  39.1 us (18%)
  starting transfers between devices  30.8 us (14%)
  waiting for transfers between devices  30.5 us (14%)
    dot_general x3, matrix products, one_block(): jnp.einsum('hrk,khd->rhd', weights, value_block, preferred_element_type=j...  26 us
    all_to_all x1, waiting for transfers between devices, attend_columns(): lax.all_to_all(output, 'frame', split_axis=0, concat_axis=1, tiled=True)  13.4 us
    select_n x3, other arithmetic, whole_frame(): jnp.where(parity == 0, jnp.concatenate([own, got], axis=0), jnp.concatena...  11.7 us
    all_to_all x1, waiting for transfers between devices, attend_columns(): lax.all_to_all(query_part[None], 'frame', split_axis=1, concat_axis=0, ti...  10.1 us
    all_to_all x1, starting transfers between devices, attend_columns(): lax.all_to_all(query_part[None], 'frame', split_axis=1, concat_axis=0, ti...  8.06 us
    all_to_all x1, starting transfers between devices, attend_columns(): lax.all_to_all(value_part[None], 'frame', split_axis=1, concat_axis=0, ti...  8.02 us
    dot_general x3, matrix products, one_block(): jnp.einsum('rhd,khd->hrk', query_block, key_block, preferred_element_type...  7.84 us
    all_to_all x1, starting transfers between devices, attend_columns(): lax.all_to_all(key_part[None], 'frame', split_axis=1, concat_axis=0, tile...  7.43 us
  transfers between devices with their start and end apart: 8, of which 4 were waited for; matrix products, arithmetic and copies ran while one was open for 46% of the time, Pallas kernels for 0%

commit v1 on v0

v1 whole, which is shorter than its diff:
```python
import functools
import math

import jax
import jax.numpy as jnp
from jax import lax
from jax.experimental import pallas as pl
from jax.experimental.pallas import tpu as pltpu
from jax.sharding import PartitionSpec as P

TEMP_HEADS = 10
UNIT = 16
SIZE = 128
F32 = jnp.float32
BF16 = jnp.bfloat16


def temporal_positions(labels, heads):
    def pick(head, carry):
        count, found = carry
        label = labels[head]
        found = tuple(
            jnp.where(label * (count + 1) == slot + 1, head, have)
            for slot, have in enumerate(found)
        )
        return count + label, found

    zero = jnp.int32(0)
    return lax.fori_loop(0, heads, pick, (zero, (zero,) * TEMP_HEADS))[1]


def cut_units(units):
    first = (units + 1) // 2
    return [(0, first), (first, units - first)]


def attend(query, key, value, scale, keep=None):
    scores = lax.dot_general(query, key, (((1,), (1,)), ((), ())), preferred_element_type=F32)
    if keep is not None:
        scores = jnp.where(keep, scores, F32(-1e30))
    peak = jnp.max(scores, axis=1, keepdims=True)
    weights = jnp.exp2((scores - peak) * F32(scale * math.log2(math.e))).astype(BF16)
    wide = jnp.concatenate([value, jnp.ones_like(value)], axis=1)
    total = jnp.dot(weights, wide, preferred_element_type=F32)
    return (total[:, :SIZE] / total[:, SIZE:]).astype(BF16)


def kernel(
    frames,
    units,
    head_band,
    packed,
    q_hbm,
    k_hbm,
    v_hbm,
    spatial_hbm,
    temporal_hbm,
    q_own,
    k_all,
    v_all,
    got,
    result,
    spatial,
    load_sem,
    pair_send,
    pair_recv,
    own_sem,
    send_sem,
    recv_sem,
    back_own,
    back_send,
    back_recv,
    out_sem,
):
    rows, width = q_own.shape
    heads = width // SIZE
    groups = rows // UNIT
    share = units * UNIT
    scale = 1.0 / math.sqrt(SIZE)
    cuts = [(start * UNIT, count * UNIT) for start, count in cut_units(units)]
    me = lax.axis_index("frame")
    frame = me // 2
    core = me % 2
    partner = {"frame": me + 1 - 2 * core}

    def peer(other):
        return {"frame": other * 2 + core}

    own_rows = pl.ds(0, rows)
    loads = [
        pltpu.make_async_copy(q_hbm, q_own, load_sem.at[0]),
        pltpu.make_async_copy(k_hbm, k_all.at[own_rows], load_sem.at[1]),
        pltpu.make_async_copy(v_hbm, v_all.at[own_rows], load_sem.at[2]),
    ]
    for load in loads:
        load.start()

    barrier = pltpu.get_barrier_semaphore()
    pl.semaphore_signal(barrier, inc=1, device_id=partner, device_id_type=pl.DeviceIdType.MESH)

    def greet(step, _):
        pl.semaphore_signal(
            barrier,
            inc=1,
            device_id=peer((frame + step) % frames),
            device_id_type=pl.DeviceIdType.MESH,
        )
        return 0

    lax.fori_loop(1, frames, greet, 0)

    pl.semaphore_wait(barrier, frames)

    def part_copy(cut, tensor, to, source):
        first, count = cuts[cut]
        return pltpu.make_async_remote_copy(
            src_ref=packed.at[tensor, pl.ds(pl.multiple_of(to * share + first, UNIT), count)],
            dst_ref=got.at[tensor, frame, pl.ds(first, count)],
            send_sem=send_sem.at[cut, tensor, to],
            recv_sem=recv_sem.at[cut, tensor, source],
            device_id=peer(to),
            device_id_type=pl.DeviceIdType.MESH,
        )

    def own_copy(tensor):
        return pltpu.make_async_copy(
            packed.at[tensor, pl.ds(pl.multiple_of(frame * share, UNIT), share)],
            got.at[tensor, frame],
            own_sem.at[tensor],
        )

    def back_copy(cut, to, source):
        first, count = cuts[cut]
        return pltpu.make_async_remote_copy(
            src_ref=result.at[to, pl.ds(first, count)],
            dst_ref=temporal_hbm.at[pl.ds(pl.multiple_of(frame * share + first, UNIT), count)],
            send_sem=back_send.at[cut, to],
            recv_sem=back_recv.at[cut, source],
            device_id=peer(to),
            device_id_type=pl.DeviceIdType.MESH,
        )

    def back_own_copy(cut):
        first, count = cuts[cut]
        return pltpu.make_async_copy(
            result.at[frame, pl.ds(first, count)],
            temporal_hbm.at[pl.ds(pl.multiple_of(frame * share + first, UNIT), count)],
            back_own.at[cut],
        )

    def over_peers(action):
        def step_action(step, _):
            action((frame + step) % frames)
            return 0

        lax.fori_loop(1, frames, step_action, 0)

    pair = []
    for tensor, held in ((1, k_all), (2, v_all)):
        pair.append(
            pltpu.make_async_remote_copy(
                src_ref=held.at[own_rows],
                dst_ref=held.at[pl.ds(rows, rows)],
                send_sem=pair_send.at[tensor - 1],
                recv_sem=pair_recv.at[tensor - 1],
                device_id=partner,
                device_id_type=pl.DeviceIdType.MESH,
            )
        )

    for tensor in range(3):
        over_peers(lambda other, tensor=tensor: part_copy(0, tensor, other, frame).start())
        own_copy(tensor).start()
    for load in loads:
        load.wait()
    for copy in pair:
        copy.start()
    for cut in range(1, len(cuts)):
        for tensor in range(3):
            over_peers(
                lambda other, cut=cut, tensor=tensor: part_copy(cut, tensor, other, frame).start()
            )
    for copy in pair:
        copy.wait()

    def one_head(head, _):
        columns = pl.ds(pl.multiple_of(head * SIZE, SIZE), SIZE)
        spatial[:, columns] = attend(
            q_own[:, columns], k_all[:, columns], v_all[:, columns], scale
        )
        return 0

    lax.fori_loop(0, heads, one_head, 0)
    out_copy = pltpu.make_async_copy(spatial, spatial_hbm, out_sem)
    out_copy.start()

    for tensor in range(3):
        own_copy(tensor).wait()
    tall = frames * UNIT
    row_id = lax.broadcasted_iota(jnp.int32, (tall, tall), 0)
    column_id = lax.broadcasted_iota(jnp.int32, (tall, tall), 1)
    distance = jnp.where(
        row_id % UNIT == column_id % UNIT, jnp.abs(row_id // UNIT - column_id // UNIT), 2 * frames
    )
    for cut, (first, count) in enumerate(cuts):
        for tensor in range(3):
            over_peers(
                lambda other, cut=cut, tensor=tensor: part_copy(
                    cut, tensor, other, other
                ).wait_recv()
            )

        def one_unit(number, _, first=first):
            start = pl.multiple_of(first + number * UNIT, UNIT)
            place = frame * units + first // UNIT + number
            reach = head_band[jnp.minimum(place // groups, TEMP_HEADS - 1)]
            parts = [got[t, :, pl.ds(start, UNIT), :].reshape(tall, SIZE) for t in range(3)]
            out = attend(*parts, scale, distance <= reach)
            result[:, pl.ds(start, UNIT), :] = out.reshape(frames, UNIT, SIZE)
            return 0

        lax.fori_loop(0, count // UNIT, one_unit, 0)
        over_peers(lambda other, cut=cut: back_copy(cut, other, frame).start())
        back_own_copy(cut).start()

    for cut in range(len(cuts)):
        back_own_copy(cut).wait()
        over_peers(lambda other, cut=cut: back_copy(cut, other, other).wait())
        for tensor in range(3):
            over_peers(
                lambda other, cut=cut, tensor=tensor: part_copy(
                    cut, tensor, other, frame
                ).wait_send()
            )
    out_copy.wait()


def pack_kernel(labels, band, q_hbm, k_hbm, v_hbm, packed, head_band, sems):
    rows, width = q_hbm.shape
    copies = []
    for slot, head in enumerate(temporal_positions(labels, width // SIZE)):
        head_band[slot] = band[head]
        for tensor, source in enumerate((q_hbm, k_hbm, v_hbm)):
            copies.append(
                pltpu.make_async_copy(
                    source.at[:, pl.ds(pl.multiple_of(head * SIZE, SIZE), SIZE)],
                    packed.at[tensor, pl.ds(slot * rows, rows)],
                    sems.at[tensor, slot],
                )
            )
            copies[-1].start()
    for copy in copies:
        copy.wait()


def place_kernel(labels, spatial_hbm, temporal_hbm, out_hbm, sems):
    rows, width = out_hbm.shape

    def spatial_copy(head):
        columns = pl.ds(pl.multiple_of(head * SIZE, SIZE), SIZE)
        return pltpu.make_async_copy(
            spatial_hbm.at[:, columns], out_hbm.at[:, columns], sems.at[head]
        )

    def start(head, count):
        label = labels[head]

        @pl.when(label == 0)
        def _():
            spatial_copy(head).start()

        @pl.when(label != 0)
        def _():
            columns = pl.ds(pl.multiple_of(head * SIZE, SIZE), SIZE)
            pltpu.make_async_copy(
                temporal_hbm.at[pl.ds(pl.multiple_of(count * rows, UNIT), rows)],
                out_hbm.at[:, columns],
                sems.at[head],
            ).start()

        return count + label

    def finish(head, _):
        spatial_copy(head).wait()
        return 0

    lax.fori_loop(0, width // SIZE, start, jnp.int32(0))
    lax.fori_loop(0, width // SIZE, finish, 0)


def shards(queries, keys, values, labels, band):
    rows, width = queries.shape
    frames = lax.axis_size("frame") // 2
    groups = rows // UNIT
    units = -(-TEMP_HEADS * groups // frames)
    share = units * UNIT
    cuts = len(cut_units(units))
    anywhere = pl.BlockSpec(memory_space=pl.ANY)
    scalars = pl.BlockSpec(memory_space=pltpu.SMEM)
    heads = width // SIZE
    dma = pltpu.SemaphoreType.DMA
    packed, head_band = pl.pallas_call(
        pack_kernel,
        out_shape=(
            jax.ShapeDtypeStruct((3, frames * share, SIZE), BF16),
            jax.ShapeDtypeStruct((TEMP_HEADS,), jnp.int32),
        ),
        in_specs=[scalars, scalars, anywhere, anywhere, anywhere],
        out_specs=(anywhere, scalars),
        scratch_shapes=[dma((3, TEMP_HEADS))],
    )(labels, band, queries, keys, values)
    spatial, temporal = pl.pallas_call(
        functools.partial(kernel, frames, units),
        out_shape=(
            jax.ShapeDtypeStruct((rows, width), BF16),
            jax.ShapeDtypeStruct((frames * share, SIZE), BF16),
        ),
        in_specs=[scalars, anywhere, anywhere, anywhere, anywhere],
        out_specs=(anywhere, anywhere),
        scratch_shapes=[
            pltpu.VMEM((rows, width), BF16),
            pltpu.VMEM((2 * rows, width), BF16),
            pltpu.VMEM((2 * rows, width), BF16),
            pltpu.VMEM((3, frames, share, SIZE), BF16),
            pltpu.VMEM((frames, share, SIZE), BF16),
            pltpu.VMEM((rows, width), BF16),
            dma((3,)),
            dma((2,)),
            dma((2,)),
            dma((3,)),
            dma((cuts, 3, frames)),
            dma((cuts, 3, frames)),
            dma((cuts,)),
            dma((cuts, frames)),
            dma((cuts, frames)),
            dma,
        ],
        compiler_params=pltpu.CompilerParams(
            collective_id=0, has_side_effects=True, vmem_limit_bytes=56 * 2**20
        ),
        cost_estimate=pl.CostEstimate(
            flops=8 * heads * rows * rows * SIZE,
            bytes_accessed=8 * rows * width,
            transcendentals=2 * heads * rows * rows,
        ),
    )(head_band, packed, queries, keys, values)
    return pl.pallas_call(
        place_kernel,
        out_shape=jax.ShapeDtypeStruct((rows, width), BF16),
        in_specs=[scalars, anywhere, anywhere],
        out_specs=anywhere,
        scratch_shapes=[dma((heads,))],
    )(labels, spatial, temporal)


def solution(mesh):
    placed = (
        P(("group", "frame"), None),
        P(("group", "frame"), None),
        P(("group", "frame"), None),
        P("group"),
        P("group"),
    )
    return jax.shard_map(
        shards, mesh=mesh, in_specs=placed, out_specs=P(("group", "frame"), None), check_vma=False
    )
```

time: 213 us -> 258 us (1.21)
  Pallas kernels: 0 us -> 258 us
  local copies, waits for them, and re-layouts: 71.1 us -> 0 us
  matrix products: 39.9 us -> 0 us
  other arithmetic: 39.1 us -> 0 us
  starting transfers between devices: 30.8 us -> 0 us
  waiting for transfers between devices: 30.5 us -> 0 us
    pallas_call x0 -> x3, Pallas kernels: none -> 258 us  [the longest x1 101 us: shards(): pl.pallas_call(place_kernel, out_shape=jax.ShapeDtypeStruct((rows, width)...]
    dot_general x7 -> x0, matrix products: 35.7 us -> none  [the longest x3 26 us: one_block(): jnp.einsum('hrk,khd->rhd', weights, value_block, preferred_element_type=j...]
    all_to_all x4 -> x0, waiting for transfers between devices: 29.9 us -> none  [the longest x1 13.4 us: attend_columns(): lax.all_to_all(output, 'frame', split_axis=0, concat_axis=1, tiled=True)]
    all_to_all x4 -> x0, starting transfers between devices: 29.6 us -> none  [the longest x1 8.06 us: attend_columns(): lax.all_to_all(query_part[None], 'frame', split_axis=1, concat_axis=0, ti...]
    gather x8 -> x0, local copies, waits for them, and re-layouts: 25.3 us -> none  [the longest x1 4.91 us: shards(): jnp.take(jnp.concatenate([spatial, temporal], axis=1), inverse, axis=1)]
    select_n x8 -> x0, other arithmetic: 23.4 us -> none  [the longest x3 11.7 us: whole_frame(): jnp.where(parity == 0, jnp.concatenate([own, got], axis=0), jnp.concatena...]
    reshape x4 -> x0, local copies, waits for them, and re-layouts: 13.1 us -> none  [the longest x1 4.66 us: shards(): key_heads = keys.reshape(row_count, head_count, head_size)]
    broadcast_in_dim x5 -> x0, local copies, waits for them, and re-layouts: 8.22 us -> none  [the longest x1 2.82 us: attend_columns(): value_part[None]]
  transfers between devices with their start and end apart: 8 -> 0, of which waited for: 4 -> 0; matrix products, arithmetic and copies ran while one was open for 46% -> 0% of each run, Pallas kernels for 0% -> 0%
where the time goes in v1:
time: 258 us
  Pallas kernels  258 us (100%)
    pallas_call x1, Pallas kernels, shards(): pl.pallas_call(place_kernel, out_shape=jax.ShapeDtypeStruct((rows, width)...  101 us
    pallas_call x1, Pallas kernels, shards(): pl.pallas_call(functools.partial(kernel, frames, units), out_shape=(jax.S...  78.8 us
    pallas_call x1, Pallas kernels, shards(): pl.pallas_call(pack_kernel, out_shape=(jax.ShapeDtypeStruct((3, frames *...  77.8 us

profile of v1, /device:TPU:0, one launch (start us, length us, event | category | flops | bytes accessed | tf_op | source)
XLA Modules:
  0.0 258.1 jit_solution(2464781934470220042)
XLA Ops:
  0.0 77.8 %shard_map.55 = (bf16[3,3200,128]{2,1,0:T(8,128)(2,1)}, s32[10]{0:T(128)}) custom-call(s32[40]{0:T(128)} %labels.3, s32[40]{0:T(128)} %band.1, bf16[320,5120]{1,0:T(8,128)(2,1)} %q_hbm.3, bf16[320,5120]{1,0:T(8,128)(2,1)} %k_hbm.3, bf16[320,5120]{1,0:T(8,128)(2,1)} %v_hbm.3), custom_call_target="tpu_custom_call" | custom-call | tf_op jit(solution)/shard_map/pallas_call | solution.py:302
  77.8 78.8 %shard_map.56 = (bf16[320,5120]{1,0:T(8,128)(2,1)}, bf16[3200,128]{1,0:T(8,128)(2,1)}) custom-call(s32[10]{0:T(128)} %get-tuple-element.9.head_band, bf16[3,3200,128]{2,1,0:T(8,128)(2,1)} %get-tuple-element.10.packed, bf16[320,5120]{1,0:T(8,128)(2,1)} %q_hbm.3, bf16[320,5120]{1,0:T(8,128)(2,1)} %k_hbm.3, bf16[320,5120]{1,0:T(8,128)(2,1)} %v_hbm.3), custom_call_target="tpu_custom_call" | custom-call | flops 4194304000 | bytes 13107200 | tf_op jit(solution)/shard_map/pallas_call | solution.py:312
  156.7 101.4 %shard_map.57 = bf16[320,5120]{1,0:T(8,128)(2,1)} custom-call(s32[40]{0:T(128)} %labels.3, bf16[320,5120]{1,0:T(8,128)(2,1)} %get-tuple-element.11.spatial_hbm, bf16[3200,128]{1,0:T(8,128)(2,1)} %get-tuple-element.12.temporal_hbm), custom_call_target="tpu_custom_call" | custom-call | tf_op jit(solution)/shard_map/pallas_call | solution.py:347

commit v2 on v1

--- a/solution.py
+++ b/solution.py
@@ -253,39 +253,15 @@
         copy.wait()
 
 
-def place_kernel(labels, spatial_hbm, temporal_hbm, out_hbm, sems):
-    rows, width = out_hbm.shape
-
-    def spatial_copy(head):
-        columns = pl.ds(pl.multiple_of(head * SIZE, SIZE), SIZE)
-        return pltpu.make_async_copy(
-            spatial_hbm.at[:, columns], out_hbm.at[:, columns], sems.at[head]
-        )
-
-    def start(head, count):
-        label = labels[head]
-
-        @pl.when(label == 0)
-        def _():
-            spatial_copy(head).start()
-
-        @pl.when(label != 0)
-        def _():
-            columns = pl.ds(pl.multiple_of(head * SIZE, SIZE), SIZE)
-            pltpu.make_async_copy(
-                temporal_hbm.at[pl.ds(pl.multiple_of(count * rows, UNIT), rows)],
-                out_hbm.at[:, columns],
-                sems.at[head],
-            ).start()
-
-        return count + label
-
-    def finish(head, _):
-        spatial_copy(head).wait()
-        return 0
-
-    lax.fori_loop(0, width // SIZE, start, jnp.int32(0))
-    lax.fori_loop(0, width // SIZE, finish, 0)
+def place_kernel(labels, spatial, temporal, out):
+    out[...] = spatial[...]
+    heads = out.shape[1] // SIZE
+    for slot, head in enumerate(temporal_positions(labels, heads)):
+        out[:, pl.ds(pl.multiple_of(head * SIZE, SIZE), SIZE)] = temporal[slot]
+
+
+def place_rows(rows):
+    return next(count for count in (160, 128, 64, 32, 16) if rows % count == 0)
 
 
 def shards(queries, keys, values, labels, band):
@@ -306,8 +282,9 @@
             jax.ShapeDtypeStruct((TEMP_HEADS,), jnp.int32),
         ),
         in_specs=[scalars, scalars, anywhere, anywhere, anywhere],
-        out_specs=(anywhere, scalars),
+        out_specs=(pl.BlockSpec(memory_space=pltpu.VMEM), scalars),
         scratch_shapes=[dma((3, TEMP_HEADS))],
+        compiler_params=pltpu.CompilerParams(vmem_limit_bytes=24 * 2**20),
     )(labels, band, queries, keys, values)
     spatial, temporal = pl.pallas_call(
         functools.partial(kernel, frames, units),
@@ -344,13 +321,19 @@
             transcendentals=2 * heads * rows * rows,
         ),
     )(head_band, packed, queries, keys, values)
+    block = place_rows(rows)
     return pl.pallas_call(
         place_kernel,
+        grid=(rows // block,),
         out_shape=jax.ShapeDtypeStruct((rows, width), BF16),
-        in_specs=[scalars, anywhere, anywhere],
-        out_specs=anywhere,
-        scratch_shapes=[dma((heads,))],
-    )(labels, spatial, temporal)
+        in_specs=[
+            scalars,
+            pl.BlockSpec((block, width), lambda step: (step, 0)),
+            pl.BlockSpec((TEMP_HEADS, block, SIZE), lambda step: (0, step, 0)),
+        ],
+        out_specs=pl.BlockSpec((block, width), lambda step: (step, 0)),
+        compiler_params=pltpu.CompilerParams(vmem_limit_bytes=24 * 2**20),
+    )(labels, spatial, temporal[: TEMP_HEADS * rows].reshape(TEMP_HEADS, rows, SIZE))
 
 
 def solution(mesh):

time: 258 us -> 98.1 us (0.38)
  Pallas kernels: 258 us -> 85.6 us
  local copies, waits for them, and re-layouts: 0 us -> 12.1 us
    pallas_call x1, Pallas kernels: 101 us -> 3.77 us  [shards(): pl.pallas_call(place_kernel, grid=(rows // block,), out_shape=jax.ShapeDt...]
    pallas_call x1, Pallas kernels: 77.8 us -> 2.94 us  [shards(): pl.pallas_call(pack_kernel, out_shape=(jax.ShapeDtypeStruct((3, frames *...]
    unnamed x0 -> x20, local copies, waits for them, and re-layouts: none -> 12.1 us
where the time goes in v2:
time: 98.1 us; the launch traced here: 97.8 us
  Pallas kernels  85.6 us (87%)
  local copies, waits for them, and re-layouts  12.1 us (12%)
    pallas_call x1, Pallas kernels, shards(): pl.pallas_call(functools.partial(kernel, frames, units), out_shape=(jax.S...  78.9 us
    unnamed x20, local copies, waits for them, and re-layouts  12.1 us
    pallas_call x1, Pallas kernels, shards(): pl.pallas_call(place_kernel, grid=(rows // block,), out_shape=jax.ShapeDt...  3.77 us
    pallas_call x1, Pallas kernels, shards(): pl.pallas_call(pack_kernel, out_shape=(jax.ShapeDtypeStruct((3, frames *...  2.94 us

profile of v2, /device:TPU:0, one launch (start us, length us, event | category | flops | bytes accessed | tf_op | source)
XLA Modules:
  0.0 97.8 jit_solution(17551054671592447915)
XLA Ops:
  0.0 0.0 copy-start
  0.0 1.9 %copy-done = bf16[320,5120]{1,0:T(8,128)(2,1)S(1)} copy-done((bf16[320,5120]{1,0:T(8,128)(2,1)S(1)}, bf16[320,5120]{1,0:T(8,128)(2,1)}, u32[]{:S(2)}) %copy-start) | copy-done | bytes 3276824
  1.9 0.0 copy-start.1
  1.9 1.9 %copy-done.1 = bf16[320,5120]{1,0:T(8,128)(2,1)S(1)} copy-done((bf16[320,5120]{1,0:T(8,128)(2,1)S(1)}, bf16[320,5120]{1,0:T(8,128)(2,1)}, u32[]{:S(2)}) %copy-start.1) | copy-done | bytes 3276824
  3.9 0.0 copy-start.2
  3.9 1.9 %copy-done.2 = bf16[320,5120]{1,0:T(8,128)(2,1)S(1)} copy-done((bf16[320,5120]{1,0:T(8,128)(2,1)S(1)}, bf16[320,5120]{1,0:T(8,128)(2,1)}, u32[]{:S(2)}) %copy-start.2) | copy-done | bytes 3276824
  5.8 0.0 copy-start.5
  5.8 0.7 copy-done.5
  6.4 0.0 copy-start.7
  6.4 0.7 copy-done.7
  7.1 2.9 %shard_map.55 = (bf16[3,3200,128]{2,1,0:T(8,128)(2,1)S(1)}, s32[10]{0:T(128)S(1)}) custom-call(s32[40]{0:T(128)S(1)} %copy-done.5, s32[40]{0:T(128)S(1)} %copy-done.7, bf16[320,5120]{1,0:T(8,128)(2,1)S(1)} %copy-done, bf16[320,5120]{1,0:T(8,128)(2,1)S(1)} %copy-done.1, bf16[320,5120]{1,0:T(8,128)(2,1)S(1)} %copy-done.2), custom_call_target="tpu_custom_call" | custom-call | tf_op jit(solution)/shard_map/pallas_call | solution.py:278
  10.0 0.0 copy-start.8
  10.1 1.4 %copy-done.8 = bf16[3,3200,128]{2,1,0:T(8,128)(2,1)} copy-done((bf16[3,3200,128]{2,1,0:T(8,128)(2,1)}, bf16[3,3200,128]{2,1,0:T(8,128)(2,1)S(1)}, u32[]{:S(2)}) %copy-start.8) | copy-done | bytes 2457624
  11.5 0.0 copy-start.9
  11.5 0.5 copy-done.9
  12.0 0.0 copy-start.6
  12.0 78.9 %shard_map.56 = (bf16[320,5120]{1,0:T(8,128)(2,1)}, bf16[3200,128]{1,0:T(8,128)(2,1)}) custom-call(s32[10]{0:T(128)} %copy-done.9, bf16[3,3200,128]{2,1,0:T(8,128)(2,1)} %copy-done.8, bf16[320,5120]{1,0:T(8,128)(2,1)} %q_hbm.3, bf16[320,5120]{1,0:T(8,128)(2,1)} %k_hbm.3, bf16[320,5120]{1,0:T(8,128)(2,1)} %v_hbm.3), custom_call_target="tpu_custom_call" | custom-call | flops 4194304000 | bytes 13107200 | tf_op jit(solution)/shard_map/pallas_call | solution.py:289
  90.9 0.0 copy-done.6
  91.0 0.0 copy-start.3
  91.0 1.9 %copy-done.3 = bf16[320,5120]{1,0:T(8,128)(2,1)S(1)} copy-done((bf16[320,5120]{1,0:T(8,128)(2,1)S(1)}, bf16[320,5120]{1,0:T(8,128)(2,1)}, u32[]{:S(2)}) %copy-start.3) | copy-done | bytes 3276824
  92.9 0.0 copy-start.4
  92.9 1.1 %copy-done.4 = bf16[3200,128]{1,0:T(8,128)(2,1)S(1)} copy-done((bf16[3200,128]{1,0:T(8,128)(2,1)S(1)}, bf16[3200,128]{1,0:T(8,128)(2,1)}, u32[]{:S(2)}) %copy-start.4) | copy-done | bytes 819224
  94.0 3.8 %shard_map.57 = bf16[320,5120]{1,0:T(8,128)(2,1)} custom-call(s32[40]{0:T(128)S(1)} %copy-done.6, bf16[320,5120]{1,0:T(8,128)(2,1)S(1)} %copy-done.3, bf16[10,320,128]{2,1,0:T(8,128)(2,1)S(1)} %bitcast.1), custom_call_target="tpu_custom_call" | custom-call | tf_op jit(solution)/shard_map/pallas_call | solution.py:325
Async XLA Ops:
  0.0 1.9 %copy-start = (bf16[320,5120]{1,0:T(8,128)(2,1)S(1)}, bf16[320,5120]{1,0:T(8,128)(2,1)}, u32[]{:S(2)}) copy-start(bf16[320,5120]{1,0:T(8,128)(2,1)} %q_hbm.3) | copy-start | bytes 9830404
  1.9 1.9 %copy-start.1 = (bf16[320,5120]{1,0:T(8,128)(2,1)S(1)}, bf16[320,5120]{1,0:T(8,128)(2,1)}, u32[]{:S(2)}) copy-start(bf16[320,5120]{1,0:T(8,128)(2,1)} %k_hbm.3) | copy-start | bytes 9830404
  3.9 1.9 %copy-start.2 = (bf16[320,5120]{1,0:T(8,128)(2,1)S(1)}, bf16[320,5120]{1,0:T(8,128)(2,1)}, u32[]{:S(2)}) copy-start(bf16[320,5120]{1,0:T(8,128)(2,1)} %v_hbm.3) | copy-start | bytes 9830404
  5.8 0.7 copy-start.5
  6.4 0.7 copy-start.7
  10.0 1.4 %copy-start.8 = (bf16[3,3200,128]{2,1,0:T(8,128)(2,1)}, bf16[3,3200,128]{2,1,0:T(8,128)(2,1)S(1)}, u32[]{:S(2)}) copy-start(bf16[3,3200,128]{2,1,0:T(8,128)(2,1)S(1)} %get-tuple-element.10.packed) | copy-start | bytes 7372804
  11.5 0.5 copy-start.9
  12.0 78.9 %copy-start.6 = (s32[40]{0:T(128)S(1)}, s32[40]{0:T(128)}, u32[]{:S(2)}) copy-start(s32[40]{0:T(128)} %labels.3) | copy-start | bytes 484
  91.0 1.9 %copy-start.3 = (bf16[320,5120]{1,0:T(8,128)(2,1)S(1)}, bf16[320,5120]{1,0:T(8,128)(2,1)}, u32[]{:S(2)}) copy-start(bf16[320,5120]{1,0:T(8,128)(2,1)} %get-tuple-element.11.spatial) | copy-start | bytes 9830404
  92.9 1.1 %copy-start.4 = (bf16[3200,128]{1,0:T(8,128)(2,1)S(1)}, bf16[3200,128]{1,0:T(8,128)(2,1)}, u32[]{:S(2)}) copy-start(bf16[3200,128]{1,0:T(8,128)(2,1)} %get-tuple-element.12) | copy-start | bytes 2457604

commit v3 on v2

--- a/solution.py
+++ b/solution.py
@@ -10,6 +10,7 @@
 
 TEMP_HEADS = 10
 UNIT = 16
+BATCH = 4
 SIZE = 128
 F32 = jnp.float32
 BF16 = jnp.bfloat16
@@ -210,16 +211,26 @@
                 ).wait_recv()
             )
 
-        def one_unit(number, _, first=first):
+        def one_unit(number, first):
             start = pl.multiple_of(first + number * UNIT, UNIT)
             place = frame * units + first // UNIT + number
             reach = head_band[jnp.minimum(place // groups, TEMP_HEADS - 1)]
             parts = [got[t, :, pl.ds(start, UNIT), :].reshape(tall, SIZE) for t in range(3)]
             out = attend(*parts, scale, distance <= reach)
-            result[:, pl.ds(start, UNIT), :] = out.reshape(frames, UNIT, SIZE)
+            return start, out.reshape(frames, UNIT, SIZE)
+
+        def some_units(base, size, first):
+            for start, out in [one_unit(base + step, first) for step in range(size)]:
+                result[:, pl.ds(start, UNIT), :] = out
+
+        def one_batch(number, _, first=first):
+            some_units(number * BATCH, BATCH, first)
             return 0
 
-        lax.fori_loop(0, count // UNIT, one_unit, 0)
+        todo = count // UNIT
+        lax.fori_loop(0, todo // BATCH, one_batch, 0)
+        if todo % BATCH:
+            some_units(todo - todo % BATCH, todo % BATCH, first)
         over_peers(lambda other, cut=cut: back_copy(cut, other, frame).start())
         back_own_copy(cut).start()
 
@@ -235,22 +246,30 @@
     out_copy.wait()
 
 
-def pack_kernel(labels, band, q_hbm, k_hbm, v_hbm, packed, head_band, sems):
+def pack_kernel(labels, band, q_hbm, k_hbm, v_hbm, packed, head_band, held, in_sem, out_sem):
     rows, width = q_hbm.shape
+    found = temporal_positions(labels, width // SIZE)
     copies = []
-    for slot, head in enumerate(temporal_positions(labels, width // SIZE)):
+    for tensor, source in enumerate((q_hbm, k_hbm, v_hbm)):
+        for slot, head in enumerate(found):
+            copy = pltpu.make_async_copy(
+                source.at[:, pl.ds(pl.multiple_of(head * SIZE, SIZE), SIZE)],
+                held.at[tensor, pl.ds(slot * rows, rows)],
+                in_sem.at[tensor, slot],
+            )
+            copy.start()
+            part = (tensor, pl.ds(slot * rows, rows))
+            back = pltpu.make_async_copy(
+                held.at[part], packed.at[part], out_sem.at[tensor, slot]
+            )
+            copies.append((copy, back))
+    for slot, head in enumerate(found):
         head_band[slot] = band[head]
-        for tensor, source in enumerate((q_hbm, k_hbm, v_hbm)):
-            copies.append(
-                pltpu.make_async_copy(
-                    source.at[:, pl.ds(pl.multiple_of(head * SIZE, SIZE), SIZE)],
-                    packed.at[tensor, pl.ds(slot * rows, rows)],
-                    sems.at[tensor, slot],
-                )
-            )
-            copies[-1].start()
-    for copy in copies:
+    for copy, back in copies:
         copy.wait()
+        back.start()
+    for _, back in copies:
+        back.wait()
 
 
 def place_kernel(labels, spatial, temporal, out):
@@ -261,7 +280,7 @@
 
 
 def place_rows(rows):
-    return next(count for count in (160, 128, 64, 32, 16) if rows % count == 0)
+    return next(count for count in (64, 32, 16) if rows % count == 0)
 
 
 def shards(queries, keys, values, labels, band):
@@ -282,9 +301,13 @@
             jax.ShapeDtypeStruct((TEMP_HEADS,), jnp.int32),
         ),
         in_specs=[scalars, scalars, anywhere, anywhere, anywhere],
-        out_specs=(pl.BlockSpec(memory_space=pltpu.VMEM), scalars),
-        scratch_shapes=[dma((3, TEMP_HEADS))],
-        compiler_params=pltpu.CompilerParams(vmem_limit_bytes=24 * 2**20),
+        out_specs=(anywhere, scalars),
+        scratch_shapes=[
+            pltpu.VMEM((3, TEMP_HEADS * rows, SIZE), BF16),
+            dma((3, TEMP_HEADS)),
+            dma((3, TEMP_HEADS)),
+        ],
+        compiler_params=pltpu.CompilerParams(vmem_limit_bytes=56 * 2**20),
     )(labels, band, queries, keys, values)
     spatial, temporal = pl.pallas_call(
         functools.partial(kernel, frames, units),
@@ -332,7 +355,7 @@
             pl.BlockSpec((TEMP_HEADS, block, SIZE), lambda step: (0, step, 0)),
         ],
         out_specs=pl.BlockSpec((block, width), lambda step: (step, 0)),
-        compiler_params=pltpu.CompilerParams(vmem_limit_bytes=24 * 2**20),
+        compiler_params=pltpu.CompilerParams(vmem_limit_bytes=56 * 2**20),
     )(labels, spatial, temporal[: TEMP_HEADS * rows].reshape(TEMP_HEADS, rows, SIZE))
 
 

time: 98.1 us -> 91.2 us (0.930)
  local copies, waits for them, and re-layouts: 12.1 us -> 0 us
  Pallas kernels: 85.6 us -> 90.9 us
    unnamed x20 -> x0, local copies, waits for them, and re-layouts: 12.1 us -> none
    pallas_call x1, Pallas kernels: 3.77 us -> 7.3 us  [shards(): pl.pallas_call(place_kernel, grid=(rows // block,), out_shape=jax.ShapeDt...]
    pallas_call x1, Pallas kernels: 2.94 us -> 4.99 us  [shards(): pl.pallas_call(pack_kernel, out_shape=(jax.ShapeDtypeStruct((3, frames *...]
where the time goes in v3:
time: 91.2 us; the launch traced here: 90.9 us
  Pallas kernels  90.9 us (100%)
    pallas_call x1, Pallas kernels, shards(): pl.pallas_call(functools.partial(kernel, frames, units), out_shape=(jax.S...  78.6 us
    pallas_call x1, Pallas kernels, shards(): pl.pallas_call(place_kernel, grid=(rows // block,), out_shape=jax.ShapeDt...  7.3 us
    pallas_call x1, Pallas kernels, shards(): pl.pallas_call(pack_kernel, out_shape=(jax.ShapeDtypeStruct((3, frames *...  4.99 us

profile of v3, /device:TPU:0, one launch (start us, length us, event | category | flops | bytes accessed | tf_op | source)
XLA Modules:
  0.0 90.9 jit_solution(11565410322397925116)
XLA Ops:
  0.0 5.0 %shard_map.55 = (bf16[3,3200,128]{2,1,0:T(8,128)(2,1)}, s32[10]{0:T(128)}) custom-call(s32[40]{0:T(128)} %labels.3, s32[40]{0:T(128)} %band.1, bf16[320,5120]{1,0:T(8,128)(2,1)} %q_hbm.3, bf16[320,5120]{1,0:T(8,128)(2,1)} %k_hbm.3, bf16[320,5120]{1,0:T(8,128)(2,1)} %v_hbm.3), custom_call_target="tpu_custom_call" | custom-call | tf_op jit(solution)/shard_map/pallas_call | solution.py:297
  5.0 78.6 %shard_map.56 = (bf16[320,5120]{1,0:T(8,128)(2,1)}, bf16[3200,128]{1,0:T(8,128)(2,1)}) custom-call(s32[10]{0:T(128)} %get-tuple-element.9.head_band, bf16[3,3200,128]{2,1,0:T(8,128)(2,1)} %get-tuple-element.10.packed, bf16[320,5120]{1,0:T(8,128)(2,1)} %q_hbm.3, bf16[320,5120]{1,0:T(8,128)(2,1)} %k_hbm.3, bf16[320,5120]{1,0:T(8,128)(2,1)} %v_hbm.3), custom_call_target="tpu_custom_call" | custom-call | flops 4194304000 | bytes 13107200 | tf_op jit(solution)/shard_map/pallas_call | solution.py:312
  83.6 7.3 %shard_map.57 = bf16[320,5120]{1,0:T(8,128)(2,1)} custom-call(s32[40]{0:T(128)} %labels.3, bf16[320,5120]{1,0:T(8,128)(2,1)} %get-tuple-element.11.spatial, bf16[10,320,128]{2,1,0:T(8,128)(2,1)} %bitcast.1), custom_call_target="tpu_custom_call" | custom-call | tf_op jit(solution)/shard_map/pallas_call | solution.py:348

commit v4 on v3

--- a/solution.py
+++ b/solution.py
@@ -10,29 +10,22 @@
 
 TEMP_HEADS = 10
 UNIT = 16
+CUTS = (13, 12)
 BATCH = 4
 SIZE = 128
 F32 = jnp.float32
 BF16 = jnp.bfloat16
 
 
-def temporal_positions(labels, heads):
-    def pick(head, carry):
-        count, found = carry
-        label = labels[head]
-        found = tuple(
-            jnp.where(label * (count + 1) == slot + 1, head, have)
-            for slot, have in enumerate(found)
-        )
-        return count + label, found
-
-    zero = jnp.int32(0)
-    return lax.fori_loop(0, heads, pick, (zero, (zero,) * TEMP_HEADS))[1]
-
-
 def cut_units(units):
-    first = (units + 1) // 2
-    return [(0, first), (first, units - first)]
+    cuts, start = [], 0
+    for number, weight in enumerate(CUTS):
+        left = units - start
+        size = left if number == len(CUTS) - 1 else min(left, -(-units * weight // sum(CUTS)))
+        if size:
+            cuts.append((start, size))
+        start += size
+    return cuts
 
 
 def attend(query, key, value, scale, keep=None):
@@ -246,12 +239,18 @@
     out_copy.wait()
 
 
-def pack_kernel(labels, band, q_hbm, k_hbm, v_hbm, packed, head_band, held, in_sem, out_sem):
+def pack_kernel(labels, band, q_hbm, k_hbm, v_hbm, packed, head_band, found, held, in_sem, out_sem):
     rows, width = q_hbm.shape
-    found = temporal_positions(labels, width // SIZE)
+
+    def pick(head, count):
+        found[count] = head
+        return count + labels[head]
+
+    lax.fori_loop(0, width // SIZE, pick, jnp.int32(0), unroll=True)
     copies = []
     for tensor, source in enumerate((q_hbm, k_hbm, v_hbm)):
-        for slot, head in enumerate(found):
+        for slot in range(TEMP_HEADS):
+            head = found[slot]
             copy = pltpu.make_async_copy(
                 source.at[:, pl.ds(pl.multiple_of(head * SIZE, SIZE), SIZE)],
                 held.at[tensor, pl.ds(slot * rows, rows)],
@@ -263,8 +262,8 @@
                 held.at[part], packed.at[part], out_sem.at[tensor, slot]
             )
             copies.append((copy, back))
-    for slot, head in enumerate(found):
-        head_band[slot] = band[head]
+    for slot in range(TEMP_HEADS):
+        head_band[slot] = band[found[slot]]
     for copy, back in copies:
         copy.wait()
         back.start()
@@ -272,15 +271,38 @@
         back.wait()
 
 
-def place_kernel(labels, spatial, temporal, out):
-    out[...] = spatial[...]
-    heads = out.shape[1] // SIZE
-    for slot, head in enumerate(temporal_positions(labels, heads)):
-        out[:, pl.ds(pl.multiple_of(head * SIZE, SIZE), SIZE)] = temporal[slot]
-
-
-def place_rows(rows):
-    return next(count for count in (64, 32, 16) if rows % count == 0)
+def place_kernel(found, spatial_hbm, temporal_hbm, out_hbm, held, temporal, first_sem, in_sem, out_sem):
+    rows = held.shape[0]
+    blocks = in_sem.shape[0]
+    block = rows // blocks
+    parts = [pl.ds(number * block, block) for number in range(blocks)]
+    arrive = pltpu.make_async_copy(
+        temporal_hbm.at[pl.ds(0, TEMP_HEADS * rows)], temporal, first_sem
+    )
+    arrive.start()
+    loads = [
+        pltpu.make_async_copy(spatial_hbm.at[part], held.at[part], in_sem.at[number])
+        for number, part in enumerate(parts)
+    ]
+    stores = [
+        pltpu.make_async_copy(held.at[part], out_hbm.at[part], out_sem.at[number])
+        for number, part in enumerate(parts)
+    ]
+    for load in loads:
+        load.start()
+    arrive.wait()
+    for number, part in enumerate(parts):
+        loads[number].wait()
+        for slot in range(TEMP_HEADS):
+            columns = pl.ds(pl.multiple_of(found[slot] * SIZE, SIZE), SIZE)
+            held[part, columns] = temporal[pl.ds(slot * rows + number * block, block)]
+        stores[number].start()
+    for store in stores:
+        store.wait()
+
+
+def place_blocks(rows):
+    return next(count for count in (5, 4, 2, 1) if rows % (count * UNIT) == 0)
 
 
 def shards(queries, keys, values, labels, band):
@@ -294,14 +316,15 @@
     scalars = pl.BlockSpec(memory_space=pltpu.SMEM)
     heads = width // SIZE
     dma = pltpu.SemaphoreType.DMA
-    packed, head_band = pl.pallas_call(
+    packed, head_band, found = pl.pallas_call(
         pack_kernel,
         out_shape=(
             jax.ShapeDtypeStruct((3, frames * share, SIZE), BF16),
             jax.ShapeDtypeStruct((TEMP_HEADS,), jnp.int32),
+            jax.ShapeDtypeStruct((TEMP_HEADS + 1,), jnp.int32),
         ),
         in_specs=[scalars, scalars, anywhere, anywhere, anywhere],
-        out_specs=(anywhere, scalars),
+        out_specs=(anywhere, scalars, scalars),
         scratch_shapes=[
             pltpu.VMEM((3, TEMP_HEADS * rows, SIZE), BF16),
             dma((3, TEMP_HEADS)),
@@ -344,19 +367,21 @@
             transcendentals=2 * heads * rows * rows,
         ),
     )(head_band, packed, queries, keys, values)
-    block = place_rows(rows)
+    blocks = place_blocks(rows)
     return pl.pallas_call(
         place_kernel,
-        grid=(rows // block,),
         out_shape=jax.ShapeDtypeStruct((rows, width), BF16),
-        in_specs=[
-            scalars,
-            pl.BlockSpec((block, width), lambda step: (step, 0)),
-            pl.BlockSpec((TEMP_HEADS, block, SIZE), lambda step: (0, step, 0)),
+        in_specs=[scalars, anywhere, anywhere],
+        out_specs=anywhere,
+        scratch_shapes=[
+            pltpu.VMEM((rows, width), BF16),
+            pltpu.VMEM((TEMP_HEADS * rows, SIZE), BF16),
+            dma,
+            dma((blocks,)),
+            dma((blocks,)),
         ],
-        out_specs=pl.BlockSpec((block, width), lambda step: (step, 0)),
         compiler_params=pltpu.CompilerParams(vmem_limit_bytes=56 * 2**20),
-    )(labels, spatial, temporal[: TEMP_HEADS * rows].reshape(TEMP_HEADS, rows, SIZE))
+    )(found, spatial, temporal)
 
 
 def solution(mesh):

time: 91.2 us -> 87.5 us (0.959)
  Pallas kernels: 90.9 us -> 87.2 us
    pallas_call x1, Pallas kernels: 7.3 us -> 4.43 us  [shards(): pl.pallas_call(place_kernel, out_shape=jax.ShapeDtypeStruct((rows, width)...]
where the time goes in v4:
time: 87.5 us; the launch traced here: 87.3 us
  Pallas kernels  87.2 us (100%)
    pallas_call x1, Pallas kernels, shards(): pl.pallas_call(functools.partial(kernel, frames, units), out_shape=(jax.S...  78.6 us
    pallas_call x1, Pallas kernels, shards(): pl.pallas_call(place_kernel, out_shape=jax.ShapeDtypeStruct((rows, width)...  4.43 us
    pallas_call x1, Pallas kernels, shards(): pl.pallas_call(pack_kernel, out_shape=(jax.ShapeDtypeStruct((3, frames *...  4.23 us

profile of v4, /device:TPU:0, one launch (start us, length us, event | category | flops | bytes accessed | tf_op | source)
XLA Modules:
  0.0 87.3 jit_solution(17445827404263941429)
XLA Ops:
  0.0 4.2 %shard_map.55 = (bf16[3,3200,128]{2,1,0:T(8,128)(2,1)}, s32[10]{0:T(128)}, s32[11]{0:T(128)}) custom-call(s32[40]{0:T(128)} %labels.1, s32[40]{0:T(128)} %band.1, bf16[320,5120]{1,0:T(8,128)(2,1)} %q_hbm.3, bf16[320,5120]{1,0:T(8,128)(2,1)} %k_hbm.3, bf16[320,5120]{1,0:T(8,128)(2,1)} %v_hbm.3), custom_call_target="tpu_custom_call" | custom-call | tf_op jit(solution)/shard_map/pallas_call | solution.py:319
  4.2 78.6 %shard_map.56 = (bf16[320,5120]{1,0:T(8,128)(2,1)}, bf16[3200,128]{1,0:T(8,128)(2,1)}) custom-call(s32[10]{0:T(128)} %get-tuple-element.11.head_band, bf16[3,3200,128]{2,1,0:T(8,128)(2,1)} %get-tuple-element.12.packed, bf16[320,5120]{1,0:T(8,128)(2,1)} %q_hbm.3, bf16[320,5120]{1,0:T(8,128)(2,1)} %k_hbm.3, bf16[320,5120]{1,0:T(8,128)(2,1)} %v_hbm.3), custom_call_target="tpu_custom_call" | custom-call | flops 4194304000 | bytes 13107200 | tf_op jit(solution)/shard_map/pallas_call | solution.py:335
  82.8 4.4 %shard_map.57 = bf16[320,5120]{1,0:T(8,128)(2,1)} custom-call(s32[11]{0:T(128)} %get-tuple-element.10.found, bf16[320,5120]{1,0:T(8,128)(2,1)} %get-tuple-element.13.spatial_hbm, bf16[3200,128]{1,0:T(8,128)(2,1)} %get-tuple-element.14.temporal_hbm), custom_call_target="tpu_custom_call" | custom-call | tf_op jit(solution)/shard_map/pallas_call | solution.py:371
